TPU v7x, 32 devices: a whole 2x2x4 slice. The times are simulated.
32 devices in a mesh: dp: 4 (over y, x), fsdp: 8 (over z, core).
Axes of the slice: x: 2, y: 2, z: 4, core: 2. Of those that a mesh axis runs over, the one named last changes fastest.
Arguments:
- tokens: bfloat16 [96, 256, 1152], P(('dp', 'fsdp')), may hold values from -6 to 6
- timesteps: int32 [96], P(('dp', 'fsdp')), may hold values from 0 to 999
- labels: int32 [96], P(('dp', 'fsdp')), may hold values from 0 to 999
- head_mask: int32 [96, 16], P(('dp', 'fsdp')), may hold values 0 or 1
- keep_mask: int32 [96, 256], P(('dp', 'fsdp')), may hold values from 0 to 1, as said below
- cotangent: bfloat16 [96, 256, 1152], P(('dp', 'fsdp')), may hold values from -6 to 6
- time_weight: bfloat16 [256, 1152], P('fsdp'), may hold values from -0.375 to 0.375
- class_table: bfloat16 [1000, 1152], P(None, 'fsdp'), may hold values from -6 to 6
- ada_weight: bfloat16 [1152, 6912], P(None, 'fsdp'), may hold values from -0.1875 to 0.1875
- head_router: bfloat16 [1152, 16], P('fsdp'), may hold values from -0.1875 to 0.1875
- qkv_weight: bfloat16 [1152, 3456], P('fsdp'), may hold values from -0.1875 to 0.1875
- proj_weight: bfloat16 [1152, 1152], P('fsdp'), may hold values from -0.5 to 0.5
- fc1_weight: bfloat16 [1152, 4608], P('fsdp'), may hold values from -0.1875 to 0.1875
- fc2_weight: bfloat16 [4608, 1152], P('fsdp'), may hold values from -0.1875 to 0.1875
- token_router: bfloat16 [1152, 1], P('fsdp'), may hold values from -0.1875 to 0.1875
Outputs:
- output: bfloat16 [96, 256, 1152], P(('dp', 'fsdp'))
- grad_tokens: float32 [96, 256, 1152], P(('dp', 'fsdp'))
- grad_time_weight: float32 [256, 1152], P('fsdp')
- grad_class_table: float32 [1000, 1152], P(None, 'fsdp')
- grad_ada_weight: float32 [1152, 6912], P(None, 'fsdp')
- grad_head_router: float32 [1152, 16], P('fsdp')
- grad_qkv_weight: float32 [1152, 3456], P('fsdp')
- grad_proj_weight: float32 [1152, 1152], P('fsdp')
- grad_fc1_weight: float32 [1152, 4608], P('fsdp')
- grad_fc2_weight: float32 [4608, 1152], P('fsdp')
- grad_token_router: float32 [1152, 1], P('fsdp')
Inputs may be any that keep to these rules, and one draw needn't show every extreme that they name: `keep_mask`: each image keeps between one fifth (rounded up) and all of its 256 tokens.
All inputs are finite; a program needn't handle non-finite values. No bound on the sum of `head_mask` on one device may be relied on, other than what follows from the above.
Results may differ from a plain program's by a relative error of at most 0.02.
Values may be sent and summed in bfloat16 or wider, within the bound.
A program may use at most 256 MiB of HBM per device.

v0:
```python
from functools import partial
import math

import jax
import jax.numpy as jnp
from jax import lax
from jax.experimental import pallas as pl
from jax.experimental.pallas import tpu as pltpu
from jax.sharding import PartitionSpec as P

EPSILON = 1e-06
MESH = pl.DeviceIdType.MESH
QUARTERS = 4
DIGIT = 256


def sinusoid(steps, entries):
    half = entries // 2
    freqs = jnp.exp(-math.log(10000.0) * jnp.arange(half, dtype=jnp.float32) / half)
    angles = steps.astype(jnp.float32)[:, None] * freqs[None, :]
    return jnp.concatenate([jnp.cos(angles), jnp.sin(angles)], axis=1)


def layer_norm(value):
    centered = value - jnp.mean(value, axis=-1, keepdims=True)
    return centered * lax.rsqrt(jnp.mean(centered * centered, axis=-1, keepdims=True) + EPSILON)


def norm_back(value, grad):
    _, pull = jax.vjp(layer_norm, value)
    return pull(grad)[0]


def matmul(left, right):
    return jnp.dot(left, right, preferred_element_type=jnp.float32)


def times_rows(left, right):
    return lax.dot_general(
        left, right, (((0,), (0,)), ((), ())), preferred_element_type=jnp.float32
    )


def times_back(left, right):
    return lax.dot_general(
        left, right, (((1,), (1,)), ((), ())), preferred_element_type=jnp.float32
    )


class Place:
    def __init__(self, dp, fsdp):
        ring = fsdp // 2
        self.dp, self.fsdp, self.ring = dp, fsdp, ring
        d = lax.axis_index("dp")
        f = lax.axis_index("fsdp")
        self.d, self.f = d, f
        self.z = f // 2
        self.c = f % 2
        self.q = d % QUARTERS
        dx = d + 1 - 2 * (d % 2)
        dy = d + 2 - 4 * ((d // 2) % 2)
        self.qx = dx % QUARTERS
        self.qy = dy % QUARTERS
        self.qd = (self.qx + self.qy - self.q + QUARTERS) % QUARTERS
        self.core = (d, f + 1 - 2 * (f % 2))
        self.x = (dx, f)
        self.y = (dy, f)
        self.up = (d, ((self.z + 1) % ring) * 2 + self.c)
        self.down = (d, ((self.z + ring - 1) % ring) * 2 + self.c)

    def shard(self, back):
        return ((self.z + self.ring - back) % self.ring) * 2 + self.c

    def mates(self):
        return [(self.d, (self.f + offset) % self.fsdp) for offset in range(1, self.fsdp)]

    def cousins(self):
        return [((self.d + offset) % self.dp, self.f) for offset in range(1, self.dp)]

    def greet(self):
        barrier = pltpu.get_barrier_semaphore()
        near = self.mates() + self.cousins()
        for other in near:
            pl.semaphore_signal(barrier, inc=1, device_id=other, device_id_type=MESH)
        pl.semaphore_wait(barrier, len(near))


def remote(src, dst, send, recv, device):
    return pltpu.make_async_remote_copy(
        src_ref=src, dst_ref=dst, send_sem=send, recv_sem=recv, device_id=device, device_id_type=MESH
    )


class Swap:
    def __init__(self, partners, send, recv):
        self.partners, self.send, self.recv = partners, send, recv
        self.copies = []

    def start(self, source, landing):
        for i, device in enumerate(self.partners):
            copy = remote(source(device), landing, self.send.at[i], self.recv.at[i], device)
            copy.start()
            self.copies.append(copy)

    def arrived(self):
        for copy in self.copies:
            copy.wait_recv()

    def left(self):
        for copy in self.copies:
            copy.wait_send()


def cut(width):
    first = ((width // 128 + 1) // 2) * 128
    return (0, first), (first, width - first)


def view(ref, lead, q, width, part=None, span=None):
    start, size = (0, width) if part is None else part
    lines = slice(None) if span is None else pl.ds(*span)
    flat = ref.shape[-1] != width
    if flat:
        column = pl.multiple_of(q * width + start, 128)
        return ref.at[(*lead, lines, pl.ds(column, size))]
    return ref.at[(*lead, q, lines, pl.ds(start, size))]


def front_kernel(dp, fsdp, width, images, seq, heads, *refs):
    weights = 3
    ring = fsdp // 2
    shards, refs = refs[:weights], refs[weights:]
    ask_ref, time_ref, table_hbm, ada_hbm, router_ref, mask_ref, tokens_ref, keep_ref, cotangent_ref = refs[:9]
    refs = refs[9:]
    fulls, refs = refs[:weights], refs[weights:]
    pre_ref, mod_ref, routers_ref, all_cond_ref, all_ask_ref = refs[:5]
    h1_out, joint_out, lse_out, mixed_out, attn_out, middle_out, h2_out, active_out, slope_out = refs[5:14]
    down_out, term_out = refs[14:16]
    refs = refs[16:]
    asks, parts, mine_in, conds, columns, mods, gates = refs[:7]
    tokens, h1, joint, lse, mixed, attn, middle, h2, stage, table_ref, ada_ref, actives, slopes = refs[7:20]
    cotangent, down, term, move_sem = refs[20:24]
    refs = refs[24:]
    (own_sem, core_s, core_r, ring_s, ring_r, x_s, x_r, y_s, y_r, a_s, a_r, b_s, b_r) = refs[:13]
    mate_s, mate_r, cousin_s, cousin_r, small_sem = refs[13:]
    at = Place(dp, fsdp)
    part_a, part_b = cut(width)
    at.greet()
    sent = []
    mates, cousins = at.mates(), at.cousins()
    swaps = [Swap(mates, mate_s.at[i], mate_r.at[i]) for i in range(5)]
    far = [Swap(cousins, cousin_s.at[i], cousin_r.at[i]) for i in range(2)]
    pad = ask_ref.shape[0]
    group = fsdp * pad
    rows = table_ref.shape[0]
    spans = Reducer.halves(rows)
    chunks = shards[1].shape[1] // width

    def go(copy):
        copy.start()
        sent.append(copy)
        return copy

    def ring_copy(k, hop, half):
        index = at.shard(hop - 1)
        src = (shards[k], ()) if hop == 1 else (fulls[k], (index,))
        dst = view(fulls[k], (index,), at.q, width, span=spans[half])
        sems = ring_s.at[k, hop - 1, half], ring_r.at[k, hop - 1, half]
        return remote(view(*src, at.q, width, span=spans[half]), dst, *sems, at.up)

    small = []

    def keep(src, dst):
        copy = pltpu.make_async_copy(src, dst, small_sem.at[len(small)])
        copy.start()
        small.append(copy)

    def cond_one():
        have("table")
        swaps[0].arrived()
        asks[at.f] = ask_ref[...]
        every = asks[...].astype(jnp.float32).reshape(group, asks.shape[2])
        entries = every.shape[1] - 128
        own_rows = time_ref.shape[0]
        lanes = lax.broadcasted_iota(jnp.int32, (group, entries), 1)
        held = (lanes >= at.f * own_rows) & (lanes < (at.f + 1) * own_rows)
        embedded = jnp.where(held, every[:, :entries], 0.0).astype(jnp.bfloat16)
        stacked = jnp.concatenate([time_ref[...]] * fsdp, axis=0)
        label = (every[:, entries : entries + 1] * DIGIT + every[:, entries + 1 : entries + 2]).astype(jnp.int32)
        classes = table_ref.shape[1]
        picks = (label == lax.broadcasted_iota(jnp.int32, (group, classes), 1)).astype(jnp.float32)
        picked = times_back(picks.astype(jnp.bfloat16), table_ref[...]).astype(jnp.bfloat16)
        spot = lax.broadcasted_iota(jnp.int32, (rows, width), 1)
        line = lax.broadcasted_iota(jnp.int32, (rows, width), 0)
        place = (spot == line + at.f * rows).astype(jnp.float32).astype(jnp.bfloat16)
        partial_sum = matmul(embedded, stacked) + matmul(picked, place)
        parts[...] = partial_sum.reshape(fsdp, pad, width)
        swaps[1].start(lambda device: parts.at[device[1]], mine_in.at[at.f])

    def cond_two():
        swaps[1].arrived()
        mine_in[at.f] = parts[at.f]
        pre_cond = jnp.sum(mine_in[...], axis=0)
        pre_ref[...] = pre_cond
        conds[at.f] = (pre_cond * jax.nn.sigmoid(pre_cond)).astype(jnp.bfloat16)
        swaps[2].start(lambda device: conds.at[at.f], conds.at[at.f])

    def cond_three():
        have("ada")
        swaps[2].arrived()
        every = conds[...].astype(jnp.float32).reshape(group, width).astype(jnp.bfloat16)
        columns[...] = times_back(every, ada_ref[...]).reshape(columns.shape)
        swaps[3].start(lambda device: columns.at[device[1]], mods.at[at.f])

    def cond_four():
        swaps[3].arrived()
        swaps[4].arrived()
        mods[at.f] = columns[at.f]
        routers_ref[at.f] = router_ref[...]
        held = mods.shape[2]
        for f in range(fsdp):
            mod_ref[:, f * held : (f + 1) * held] = mods[f]
        chosen = matmul(conds[at.f], routers_ref[...].reshape(width, router_ref.shape[1]))
        gates[...] = mask_ref[...] * jax.nn.sigmoid(chosen)

    moves, moved = {}, []

    def move(name, src, dst):
        copy = pltpu.make_async_copy(src, dst, move_sem.at[len(moved)])
        copy.start()
        moved.append(copy)
        moves.setdefault(name, []).append(copy)

    def have(name):
        for copy in moves.pop(name):
            copy.wait()

    def line_of(image):
        return pl.ds(image * seq, seq)

    def bring(q):
        for f in range(fsdp):
            src = fulls[0].at[f, :, pl.ds(q * width, width)]
            move("w" + str(q), src, stage.at[q % 2, pl.ds(f * rows, rows), :])

    def modulated(image, index):
        return mod_ref[image : image + 1, index * width : (index + 1) * width]

    step = 32

    def normed(value, scale, shift):
        centered = value - jnp.mean(value, axis=-1, keepdims=True)
        inverse = lax.rsqrt(jnp.mean(centered * centered, axis=-1, keepdims=True) + EPSILON)
        return (centered * inverse * scale + shift).astype(jnp.bfloat16)

    def joint_here():
        for copy in landed[0]:
            copy.wait_recv()
        locals_[0].wait()
        bring(0)
        bring(1)

    def norm_one(image):
        if image == 0:
            have("tokens")
        shift, scale = modulated(image, 0), 1.0 + modulated(image, 1)

        @pl.loop(0, seq // step)
        def _(i):
            line = pl.ds(pl.multiple_of(image * seq + i * step, step), step)
            h1[line, :] = normed(tokens[line, :].astype(jnp.float32), scale, shift)

        if image == images - 1:
            move("h1", h1, h1_out)

    def project(q):
        have("w" + str(q))

        @pl.loop(0, images)
        def _(image):
            line = pl.ds(pl.multiple_of(image * seq, seq), seq)
            joint[line, pl.ds(q * width, width)] = matmul(h1[line, :], stage[q % 2]).astype(jnp.bfloat16)

        if q + 2 < QUARTERS:
            bring(q + 2)
        if q == 2:
            move("joint", joint, joint_out)

    def attention(image, half):
        span = range(0, heads // 2) if half == 0 else range(heads // 2, heads)
        attend_image(joint.at[line_of(image)], gates, mixed.at[line_of(image)], lse, image, seq, heads, span)
        if image == images - 1 and half == 1:
            move("mixed", mixed, mixed_out)
            move("lse", lse, lse_out)

    def merge(image):
        if image == 0:
            have("w3")
        line = line_of(image)
        attn[line, :] = matmul(mixed[line, :], stage[1])
        gate, shift, scale = modulated(image, 2), modulated(image, 3), 1.0 + modulated(image, 4)

        @pl.loop(0, seq // step)
        def _(i):
            here = pl.ds(pl.multiple_of(image * seq + i * step, step), step)
            value = tokens[here, :].astype(jnp.float32) + gate * attn[here, :]
            middle[here, :] = value
            h2[here, :] = normed(value, scale, shift)

        move("attn", attn.at[line], attn_out.at[line])
        move("middle", middle.at[line], middle_out.at[line])
        move("h2", h2.at[line], h2_out.at[line])

    def bring_fc1(c):
        for f in range(fsdp):
            src = fulls[1].at[f, :, pl.ds(c * width, width)]
            move("e" + str(c), src, stage.at[c % 2, pl.ds(f * rows, rows), :])

    def fc1_here():
        for copy in landed[1]:
            copy.wait_recv()
        locals_[1].wait()
        bring_fc1(0)
        bring_fc1(1)

    def expand(c):
        slot = c % 2
        have("e" + str(c))
        if c >= 2:
            have("active" + str(c - 2))
        bend = math.sqrt(2.0 / math.pi)
        size = 128
        pair = 2 if images * seq % (2 * size) == 0 else 1

        @pl.loop(0, images * seq // (pair * size))
        def _(i):
            for inner in range(pair):
                line = pl.ds(pl.multiple_of((i * pair + inner) * size, size), size)
                value = matmul(h2[line, :], stage[slot])
                square = value * value
                bent = jnp.tanh(value * (bend + bend * 0.044715 * square))
                half = 0.5 + 0.5 * bent
                actives[slot, line, :] = (value * half).astype(jnp.bfloat16)
                lean = value * (0.5 - 0.5 * bent * bent) * (bend + 3.0 * bend * 0.044715 * square)
                slopes[slot, line, :] = (half + lean).astype(jnp.bfloat16)

        if c + 2 < chunks:
            bring_fc1(c + 2)
        columns_of = pl.ds(c * width, width)
        move("active" + str(c), actives.at[slot], active_out.at[:, columns_of])
        move("active" + str(c), slopes.at[slot], slope_out.at[:, columns_of])

    def route(image):
        if image == 0:
            have("cotangent")
        line = line_of(image)
        chosen = matmul(h2[line, :], routers_ref[...].reshape(width, router_ref.shape[1]))
        kept = keep_ref[line, :] * jax.nn.sigmoid(chosen[:, heads : heads + 1])
        down[line, :] = (cotangent[line, :].astype(jnp.float32) * modulated(image, 5) * kept).astype(jnp.bfloat16)
        if image == images - 1:
            move("down", down, down_out)

    def weigh_fc2(c):
        if c > 0:
            have("term" + str(c - 1))

        @pl.loop(0, width // 128)
        def _(m):
            line = pl.ds(pl.multiple_of(m * 128, 128), 128)
            term[line, :] = times_rows(actives[c % 2, :, line], down[...]).astype(jnp.bfloat16)

        move("term" + str(c), term, term_out.at[pl.ds(c * width, width), :])

    move("table", table_hbm, table_ref)
    move("ada", ada_hbm, ada_ref)
    move("tokens", tokens_ref, tokens)
    move("cotangent", cotangent_ref, cotangent)
    work = [joint_here] + [partial(norm_one, image) for image in range(images)]
    work += [partial(project, q) for q in range(3)]
    work += [partial(attention, image, half) for image in range(images) for half in range(2)]
    work += [partial(merge, image) for image in range(images)] + [partial(route, image) for image in range(images)]

    def share():
        far[0].start(lambda device: conds, all_cond_ref.at[at.d])
        far[1].start(lambda device: asks, all_ask_ref.at[at.d])
        keep(conds, all_cond_ref.at[at.d])
        keep(asks, all_ask_ref.at[at.d])

    extra = {2: cond_one, 4: cond_two, 6: cond_three, 9: cond_four, 4 * (ring - 1) + 2 * LAG: share}
    swaps[0].start(lambda device: ask_ref, asks.at[at.f])
    swaps[4].start(lambda device: router_ref, routers_ref.at[at.f])

    items = [(k, hop, half) for k in range(weights) for hop in range(1, ring) for half in range(2)]
    rings = {item: go(ring_copy(*item)) for item in items[:2]}
    locals_, landed = [], [[], [], []]
    for k in range(weights):
        copy = pltpu.make_async_copy(shards[k], fulls[k].at[at.f], own_sem.at[k])
        copy.start()
        locals_.append(copy)
        landed[k].append(go(remote(shards[k], fulls[k].at[at.f], core_s.at[k, 0, 0], core_r.at[k, 0, 0], at.core)))
    flights = {}
    each = 2 * (ring - 1)
    begin, second = each + 2 * LAG - 1, 2 * each + 2 * LAG
    done = 0
    for turn in range(len(items) + 2 * LAG):
        if turn < len(items):
            k, hop, half = items[turn]
            rings[items[turn]].wait_recv()
            if turn + 2 < len(items):
                rings[items[turn + 2]] = go(ring_copy(*items[turn + 2]))
            mine = view(fulls[k], (at.shard(hop),), at.q, width, span=spans[half])
            place = (k, hop - 1, half)
            flights[turn] = (
                go(remote(mine, mine, x_s.at[place], x_r.at[place], at.x)),
                go(remote(mine, mine, y_s.at[place], y_r.at[place], at.y)),
            )
        n = turn - LAG
        if 0 <= n < len(items):
            k, hop, half = items[n]
            place = (k, hop - 1, half)
            by_x, by_y = flights[n]
            by_x.wait_recv()
            part = view(fulls[k], (at.shard(hop),), at.qx, width, part_a, spans[half])
            first = go(remote(part, part, a_s.at[place], a_r.at[place], at.y))
            by_y.wait_recv()
            part = view(fulls[k], (at.shard(hop),), at.qy, width, part_b, spans[half])
            flights[n] = (first, go(remote(part, part, b_s.at[place], b_r.at[place], at.x)))
        n = turn - 2 * LAG
        if 0 <= n < len(items):
            k, hop, half = items[n]
            for copy in flights[n]:
                copy.wait_recv()
            span = pl.ds(*spans[half])
            whole = fulls[k].at[(at.shard(hop), span) if k < 2 else (at.shard(hop), slice(None), span)]
            landed[k].append(go(remote(whole, whole, core_s.at[k, hop, half], core_r.at[k, hop, half], at.core)))
        if turn in extra:
            extra[turn]()
        if begin <= turn < second:
            upto = -(-len(work) * (turn + 1 - begin) // (second - begin))
            for part in work[done:upto]:
                part()
            done = upto
        elif turn == second:
            fc1_here()
        elif second < turn <= second + chunks:
            expand(turn - second - 1)
            weigh_fc2(turn - second - 1)
    for swap in far:
        swap.arrived()
    for copy in landed[2]:
        copy.wait_recv()
    for copy in locals_[2:] + small:
        copy.wait()
    for c in range(max(chunks - 2, 0), chunks):
        have("active" + str(c))
    have("down")
    have("term" + str(chunks - 1))
    for name in ("h1", "joint", "mixed", "lse", "attn", "middle", "h2"):
        have(name)
    for swap in swaps + far:
        swap.left()
    for copy in sent:
        copy.wait_send()


def front_half(
    shards, asked, time_weight, class_table, ada_weight, routers, mask, tokens, keep, cotangent, width, images, seq, heads,
    dp, fsdp,
):
    ring = fsdp // 2
    dma, vmem = pltpu.SemaphoreType.DMA, pltpu.VMEM
    low, f32 = jnp.bfloat16, jnp.float32
    steps = dma((3, ring - 1, 2))
    hidden = shards[1].shape[1]
    pad, asking = asked.shape
    columns = ada_weight.shape[0]
    count = images * seq
    out = jax.ShapeDtypeStruct
    any_space, in_vmem = pl.BlockSpec(memory_space=pl.ANY), pl.BlockSpec(memory_space=vmem)
    results = [
        out((count, width), low),
        out((count, 3 * width), low),
        out((images, heads, seq), f32),
        out((count, width), low),
        out((count, width), f32),
        out((count, width), f32),
        out((count, width), low),
    ]
    return pl.pallas_call(
        partial(front_kernel, dp, fsdp, width, images, seq, heads),
        out_shape=[out((fsdp, *s.shape), s.dtype) for s in shards]
        + [
            out((pad, width), f32),
            out((pad, 6 * width), f32),
            out((fsdp, *routers.shape), routers.dtype),
            out((dp, fsdp, pad, width), low),
            out((dp, fsdp, pad, asking), low),
        ]
        + results
        + [out((count, hidden), low)] * 2
        + [out((count, width), low), out((hidden, width), low)],
        in_specs=[any_space] * 3 + [in_vmem] * 2 + [any_space] * 2 + [in_vmem] * 2 + [any_space, in_vmem, any_space],
        out_specs=[any_space] * 3 + [in_vmem] * 3 + [any_space] * 13,
        scratch_shapes=[
            vmem((fsdp, pad, asking), low),
            vmem((fsdp, pad, width), f32),
            vmem((fsdp, pad, width), f32),
            vmem((fsdp, pad, width), low),
            vmem((fsdp, pad, columns), f32),
            vmem((fsdp, pad, columns), f32),
            vmem((pad, 128), f32),
            vmem((count, width), low),
        ]
        + [vmem(r.shape, r.dtype) for r in results]
        + [vmem((2, width, width), low), vmem(class_table.shape, low), vmem(ada_weight.shape, low)]
        + [vmem((2, count, width), low)] * 2
        + [vmem((count, width), low)] * 2
        + [vmem((width, width), low)]
        + [dma((8 * fsdp + 17 + 3 * images + hidden // width,))]
        + [dma((3,)), dma((3, ring, 2)), dma((3, ring, 2))]
        + [steps] * 10
        + [dma((5, fsdp - 1))] * 2
        + [dma((2, dp - 1))] * 2
        + [dma((2,))],
        compiler_params=pltpu.CompilerParams(
            collective_id=0, has_side_effects=True, vmem_limit_bytes=60 * 2**20
        ),
        name="front",
    )(*shards, asked, time_weight, class_table, ada_weight, routers, mask, tokens, keep, cotangent)


def window(head, size):
    low = head * size // 128 * 128
    high = -(-(head + 1) * size // 128) * 128
    spot = low + lax.broadcasted_iota(jnp.int32, (1, high - low), 1)
    own = ((spot >= head * size) & (spot < (head + 1) * size)).astype(jnp.float32).astype(jnp.bfloat16)
    return low, high - low, own


def attend_image(joint, gates, mixed, lse, image, seq, heads, span):
    width = mixed.shape[1]
    size = width // heads
    scale = size ** (-0.5)
    if span[0] == 0:
        mixed[...] = jnp.zeros((seq, width), mixed.dtype)
    for head in span:
        low, wide, own = window(head, size)
        query = joint[:, pl.ds(low, wide)] * own
        keys = joint[:, pl.ds(width + low, wide)]
        values = joint[:, pl.ds(2 * width + low, wide)] * own
        raw = times_back(keys, query) * scale
        peak = jnp.max(raw, axis=0, keepdims=True)
        expo = jnp.exp(raw - peak)
        total = jnp.sum(expo, axis=0, keepdims=True)
        lse[image, head : head + 1, :] = peak + jnp.log(total)
        probs = (expo * (1.0 / total)).astype(jnp.bfloat16)
        attended = times_rows(probs, values) * gates[image : image + 1, head : head + 1]
        mixed[:, pl.ds(low, wide)] = mixed[:, pl.ds(low, wide)] + attended.astype(jnp.bfloat16)


def attend_back_image(joint, grad_mixed, gates, lse, grad_joint, grad_gates, image, seq, heads, span):
    width = grad_mixed.shape[1]
    size = width // heads
    scale = size ** (-0.5)
    if span[0] == 0:
        grad_joint[...] = jnp.zeros((seq, 3 * width), grad_joint.dtype)

    def put(column, wide, value):
        here = pl.ds(column, wide)
        grad_joint[:, here] = grad_joint[:, here] + value.astype(jnp.bfloat16)

    for head in span:
        low, wide, own = window(head, size)
        query = joint[:, pl.ds(low, wide)] * own
        keys = joint[:, pl.ds(width + low, wide)] * own
        values = joint[:, pl.ds(2 * width + low, wide)]
        grad = grad_mixed[:, pl.ds(low, wide)] * own
        gate = gates[image, 0, head]
        probs = jnp.exp(times_back(keys, query) * scale - lse[image, head : head + 1, :])
        put(2 * width + low, wide, matmul(probs.astype(jnp.bfloat16), (grad.astype(jnp.float32) * gate).astype(jnp.bfloat16)))
        grad_probs = times_back(values, grad)
        inner = jnp.sum(grad_probs * probs, axis=0, keepdims=True)
        grad_gates[image, head : head + 1, :] = inner
        grad_scores = (probs * (grad_probs - inner) * (gate * scale)).astype(jnp.bfloat16)
        put(low, wide, times_rows(grad_scores, keys))
        put(width + low, wide, matmul(grad_scores, query))


def thirds(width):
    tiles = width // 128
    a, b = tiles // 3, tiles // 3
    c = tiles - a - b
    sizes = [a, b, (c + 1) // 2, c // 2]
    starts = [sum(sizes[:i]) for i in range(4)]
    return [(128 * s, 128 * n) for s, n in zip(starts, sizes)]


OWN_SLOTS = 8
PAIR_SLOTS = 4
AHEAD = 3
LAG = 2


class Reducer:
    def __init__(self, at, piece, outs, scratch, rows, width):
        self.at, self.piece, self.outs, self.width = at, piece, outs, width
        (
            self.own, self.pair, self.first_a, self.first_b, self.second_a, self.second_b,
            self.hops, self.hops_c, self.flat_a, self.flat_b, self.last_a, self.last_b, self.done,
            self.own_in, self.core_s, self.core_r, self.fa_s, self.fa_r, self.fb_s, self.fb_r,
            self.sa_s, self.sa_r, self.sb_s, self.sb_r, self.hop_s, self.hop_r, self.hopc_s, self.hopc_r,
            self.ca_s, self.ca_r, self.cb_s, self.cb_r, self.end_s, self.end_r, self.out_sem, self.credit,
        ) = scratch
        self.ring = at.ring
        self.total = 3 * self.ring * 2
        self.spans = self.halves(rows)
        self.sent, self.flights = {}, {}
        self.loose, self.outgoing = [], []
        self.cols = [pl.ds(*part) for part in thirds(width)]
        a, b = thirds(width)[1]
        self.cols_ab = pl.ds(0, a + b)
        self.cols_c = pl.ds(a + b, width - a - b)

    @staticmethod
    def halves(rows):
        top = -(-rows // 32) * 16
        return (0, top), (top, rows - top)

    def place(self, n):
        half = n % 2
        k, j = divmod(n // 2, self.ring)
        return k, j, half, self.spans[half][1]

    @staticmethod
    def scratch(rows, width, fsdp):
        ring = fsdp // 2
        total = 3 * ring * 2
        full, rows = rows, Reducer.halves(rows)[0][1]
        low, vmem, dma = jnp.bfloat16, pltpu.VMEM, pltpu.SemaphoreType.DMA
        a, b, c, d = [size for _, size in thirds(width)]
        arrays = [
            vmem((OWN_SLOTS, QUARTERS, rows, width), low),
            vmem((PAIR_SLOTS, QUARTERS, rows, width), low),
            vmem((total, 2, rows, a), low),
            vmem((total, 2, rows, b), low),
            vmem((total, rows, a), low),
            vmem((total, rows, b), low),
            vmem((3, 2, ring - 1, rows, a + b), low),
            vmem((3, 2, ring - 1, QUARTERS, rows, c + d), low),
            vmem((3, 2, 2, rows, c), low),
            vmem((3, 2, 2, rows, d), low),
            vmem((3, 2, rows, c), low),
            vmem((3, 2, rows, d), low),
            vmem((3, QUARTERS, full, width), low),
        ]
        sems = (
            [dma((total, QUARTERS))] * 3
            + [dma((total, 2))] * 4
            + [dma((total,))] * 4
            + [dma((3, 2, ring - 1))] * 4
            + [dma((3, 2, 3))] * 4
            + [dma((3, 2, 4))] * 2
            + [dma((3, 2))]
            + [pltpu.SemaphoreType.REGULAR]
        )
        return arrays + sems

    def go(self, n, *parts):
        copy = remote(*parts)
        copy.start()
        self.sent.setdefault(n, []).append(copy)
        return copy

    def prefetch(self, n):
        at = self.at
        k, j, half, size = self.place(n)
        slot, pair_slot = n % OWN_SLOTS, n % PAIR_SLOTS
        for copy in self.sent.pop(n - OWN_SLOTS, []):
            copy.wait_send()
        mine = at.shard((j + 1) % self.ring)
        other = mine + 1 - 2 * at.c
        if n >= PAIR_SLOTS:
            pl.semaphore_wait(self.credit, 1)
        brought, pairs = [], []
        span, here = pl.ds(*self.spans[half]), pl.ds(0, size)
        for q in range(QUARTERS):
            copy = pltpu.make_async_copy(self.piece(k, mine, q, span), self.own.at[slot, q, here], self.own_in.at[n, q])
            copy.start()
            brought.append(copy)
            copy = remote(
                self.piece(k, other, q, span), self.pair.at[pair_slot, q, here], self.core_s.at[n, q], self.core_r.at[n, q], at.core
            )
            copy.start()
            pairs.append(copy)
        self.loose += pairs
        self.flights[n] = (brought, pairs)

    def plane_first(self, n, slot, here, cols_a, cols_b, land_a, land_b, sems):
        at, own = self.at, self.own
        (sa, ra), (sb, rb) = sems
        return [
            self.go(n, own.at[slot, at.qd, here, cols_a], land_a.at[1, here], sa.at[1], ra.at[1], at.x),
            self.go(n, own.at[slot, at.qd, here, cols_b], land_b.at[1, here], sb.at[1], rb.at[1], at.y),
            self.go(n, own.at[slot, at.qx, here, cols_a], land_a.at[0, here], sa.at[0], ra.at[0], at.x),
            self.go(n, own.at[slot, at.qy, here, cols_b], land_b.at[0, here], sb.at[0], rb.at[0], at.y),
        ]

    def plane_second(self, n, slot, here, copies, cols_a, cols_b, land_a, land_b, next_a, next_b, sems):
        at, own = self.at, self.own
        one_d, two_d, one, two = copies
        (sa, ra), (sb, rb) = sems
        one_d.wait_recv()
        own[slot, at.qy, here, cols_a] = own[slot, at.qy, here, cols_a] + land_a[1, here]
        on_a = self.go(n, own.at[slot, at.qy, here, cols_a], next_a.at[here], sa, ra, at.y)
        two_d.wait_recv()
        own[slot, at.qx, here, cols_b] = own[slot, at.qx, here, cols_b] + land_b[1, here]
        on_b = self.go(n, own.at[slot, at.qx, here, cols_b], next_b.at[here], sb, rb, at.x)
        one.wait_recv()
        own[slot, at.q, here, cols_a] = own[slot, at.q, here, cols_a] + land_a[0, here]
        two.wait_recv()
        own[slot, at.q, here, cols_b] = own[slot, at.q, here, cols_b] + land_b[0, here]
        return [on_a, on_b]

    def plane_third(self, slot, here, copies, cols_a, cols_b, next_a, next_b):
        at, own = self.at, self.own
        for copy in copies:
            copy.wait_recv()
        own[slot, at.q, here, cols_a] = own[slot, at.q, here, cols_a] + next_a[here, :]
        own[slot, at.q, here, cols_b] = own[slot, at.q, here, cols_b] + next_b[here, :]

    def one(self, n):
        at, own, pair = self.at, self.own, self.pair
        k, j, half, size = self.place(n)
        slot, pair_slot = n % OWN_SLOTS, n % PAIR_SLOTS
        here = pl.ds(0, size)
        brought, pairs = self.flights[n]
        for q in range(QUARTERS):
            brought[q].wait()
            pairs[q].wait_recv()

        @pl.loop(0, QUARTERS)
        def _(q):
            own[slot, q, here, :] = own[slot, q, here, :] + pair[pair_slot, q, here, :]

        if n + PAIR_SLOTS < self.total:
            pl.semaphore_signal(self.credit, inc=1, device_id=at.core, device_id_type=MESH)
        a, b, c, d = self.cols
        self.flights[n] = self.plane_first(
            n, slot, here, a, b, self.first_a.at[n], self.first_b.at[n],
            ((self.fa_s.at[n], self.fa_r.at[n]), (self.fb_s.at[n], self.fb_r.at[n])),
        )
        if j > 0:
            self.flights[k, half, "c"].wait_recv()

            @pl.loop(0, QUARTERS)
            def _(q):
                own[slot, q, here, self.cols_c] = own[slot, q, here, self.cols_c] + self.hops_c[k, half, j - 1, q, here, :]

        if j < self.ring - 1:
            self.flights[k, half, "c"] = self.go(
                n, own.at[slot, slice(None), here, self.cols_c], self.hops_c.at[k, half, j, slice(None), here],
                self.hopc_s.at[k, half, j], self.hopc_r.at[k, half, j], at.up,
            )
        else:
            self.flights[k, half, "flat"] = self.plane_first(
                n, slot, here, c, d, self.flat_a.at[k, half], self.flat_b.at[k, half],
                ((self.ca_s.at[k, half], self.ca_r.at[k, half]), (self.cb_s.at[k, half], self.cb_r.at[k, half])),
            )

    def two(self, n):
        k, j, half, size = self.place(n)
        slot, here = n % OWN_SLOTS, pl.ds(0, size)
        a, b, c, d = self.cols
        self.flights[n] = self.plane_second(
            n, slot, here, self.flights[n], a, b, self.first_a.at[n], self.first_b.at[n], self.second_a.at[n], self.second_b.at[n],
            ((self.sa_s.at[n], self.sa_r.at[n]), (self.sb_s.at[n], self.sb_r.at[n])),
        )
        if j == self.ring - 1:
            self.flights[k, half, "flat"] = self.plane_second(
                n, slot, here, self.flights[k, half, "flat"], c, d, self.flat_a.at[k, half], self.flat_b.at[k, half],
                self.last_a.at[k, half], self.last_b.at[k, half],
                ((self.ca_s.at[k, half, 2], self.ca_r.at[k, half, 2]), (self.cb_s.at[k, half, 2], self.cb_r.at[k, half, 2])),
            )

    def three(self, n):
        at, own = self.at, self.own
        k, j, half, size = self.place(n)
        slot, here = n % OWN_SLOTS, pl.ds(0, size)
        a, b, c, d = self.cols
        self.plane_third(slot, here, self.flights[n], a, b, self.second_a.at[n], self.second_b.at[n])
        if j > 0:
            self.flights[k, half, "ab"].wait_recv()
            own[slot, at.q, here, self.cols_ab] = own[slot, at.q, here, self.cols_ab] + self.hops[k, half, j - 1, here, :]
        if j < self.ring - 1:
            self.flights[k, half, "ab"] = self.go(
                n, own.at[slot, at.q, here, self.cols_ab], self.hops.at[k, half, j, here],
                self.hop_s.at[k, half, j], self.hop_r.at[k, half, j], at.up,
            )
            return
        self.plane_third(slot, here, self.flights[k, half, "flat"], c, d, self.last_a.at[k, half], self.last_b.at[k, half])
        span = pl.ds(*self.spans[half])
        self.done[k, at.q, span, :] = own[slot, at.q, here, :]
        mine = self.done.at[k, at.q, span]
        sems = self.end_s.at[k, half], self.end_r.at[k, half]
        self.flights[k, half, "end"] = [
            self.keep(remote(mine, mine, sems[0].at[0], sems[1].at[0], at.x)),
            self.keep(remote(mine, mine, sems[0].at[1], sems[1].at[1], at.y)),
        ]

    def keep(self, copy):
        copy.start()
        self.loose.append(copy)
        return copy

    def four(self, n):
        at, done = self.at, self.done
        k, _, half, _ = self.place(n)
        (start_a, size_a), (start_b, size_b) = cut(self.width)
        span = pl.ds(*self.spans[half])
        sems = self.end_s.at[k, half], self.end_r.at[k, half]
        by_x, by_y = self.flights[k, half, "end"]
        by_x.wait_recv()
        part = done.at[k, at.qx, span, pl.ds(start_a, size_a)]
        first = self.keep(remote(part, part, sems[0].at[2], sems[1].at[2], at.y))
        by_y.wait_recv()
        part = done.at[k, at.qy, span, pl.ds(start_b, size_b)]
        second = self.keep(remote(part, part, sems[0].at[3], sems[1].at[3], at.x))
        self.flights[k, half, "end"] = [first, second]

    def five(self, n):
        k, _, half, _ = self.place(n)
        for copy in self.flights[k, half, "end"]:
            copy.wait_recv()
        span = pl.ds(*self.spans[half])
        copy = pltpu.make_async_copy(self.done.at[k, :, span], self.outs[k].at[:, span], self.out_sem.at[k, half])
        copy.start()
        self.outgoing.append(copy)

    def turn(self, t, starts):
        if t in starts:
            for n in range(t, t + AHEAD):
                self.prefetch(n)
        n = t + AHEAD
        if n < self.total and not any(t < start <= n for start in starts):
            self.prefetch(n)
        stages = (self.one, self.two, self.three, self.four, self.five)
        for i, stage in enumerate(stages):
            n = t - LAG * i
            if 0 <= n < self.total and (i < 3 or self.place(n)[1] == self.ring - 1):
                stage(n)

    def finish(self):
        for copy in self.outgoing:
            copy.wait()
        for copies in self.sent.values():
            for copy in copies:
                copy.wait_send()
        for copy in self.loose:
            copy.wait_send()


def back_kernel(dp, fsdp, width, images, seq, heads, *refs):
    ring = fsdp // 2
    fc2_ref, joint_ref, h1_ref, h2_ref, tokens_ref, weight_ref, down_ref, slope_ref = refs[:8]
    fc1_weight_ref, fc2_weight_ref, held_ref, attn_ref, cotangent_ref, forward_ref = refs[8:14]
    lse_ref, gates_ref, gate_two_ref, mod_ref, factor_ref, routers_ref, ada_hbm, pre_ref, picker_ref = refs[14:23]
    logit_ref, pick_ref = refs[23:25]
    refs = refs[25:]
    outs, refs = refs[:3], refs[3:]
    all_gm_ref, all_pre_ref, grad_tokens_ref, triple_ref, middle_ref, proj_ref, expand_ref = refs[:7]
    refs = refs[7:]
    joint, mixed, h1, middle, grad_joint, stage, total, inner, gm_row, gms, parts, mine_in, pres, ada_ref = refs[:14]
    in_sem, out_sem, mate_s, mate_r, cousin_s, cousin_r = refs[14:20]
    at = Place(dp, fsdp)
    at.greet()
    rows = fc1_weight_ref.shape[1]
    count = images * seq
    pad = pre_ref.shape[0]

    def piece(k, index, q, span):
        if k == 0:
            return fc2_ref.at[index, q, span]
        line = pl.ds(pl.multiple_of(index * rows + span.start, 8), span.size)
        if k == 1:
            return expand_ref.at[line, pl.ds(q * width, width)]
        if q == 3:
            return proj_ref.at[line, :]
        return triple_ref.at[q, line, :]

    work = Reducer(at, piece, outs, refs[20:], rows, width)
    moves, fetched = {}, []

    def fetch(name, src, dst):
        copy = pltpu.make_async_copy(src, dst, in_sem.at[len(fetched)])
        copy.start()
        fetched.append(copy)
        moves.setdefault(name, []).append(copy)

    def have(name):
        for copy in moves.pop(name):
            copy.wait()

    def store(name, src, dst, i):
        copy = pltpu.make_async_copy(src, dst, out_sem.at[i])
        copy.start()
        moves[name] = [copy]

    for n in range(AHEAD):
        work.prefetch(n)

    def lines(image):
        return pl.ds(image * seq, seq)

    def modulated(image, index):
        return mod_ref[image : image + 1, index * width : (index + 1) * width]

    chunks = fc1_weight_ref.shape[2] // width

    def bring_slope(c):
        fetch("s" + str(c), slope_ref.at[:, pl.ds(c * width, width)], grad_joint.at[:, pl.ds(c % 3 * width, width)])

    def bring_fc1(c):
        for f in range(fsdp):
            fetch("f" + str(c), fc1_weight_ref.at[f, :, pl.ds(c * width, width)], stage.at[0, pl.ds(f * rows, rows), :])

    def bring_fc2(c):
        for i in range(fsdp):
            f, q = c * (fsdp // chunks) + i // QUARTERS, i % QUARTERS
            fetch("d" + str(c), fc2_weight_ref.at[f, q], stage.at[2, pl.ds(i * rows, rows), :])

    def bring_image(image):
        fetch("image" + str(image), held_ref.at[lines(image)], middle.at[0])
        fetch("image" + str(image), attn_ref.at[lines(image)], middle.at[1])
        fetch("image" + str(image), cotangent_ref.at[lines(image)], joint.at[1, :, pl.ds(0, width)])

    fetch("down", down_ref, mixed)
    bring_fc2(0)
    bring_slope(0)
    fetch("h2", h2_ref, h1)
    bring_fc1(0)
    bring_slope(1)
    bring_slope(2)
    fetch("joint0", joint_ref.at[lines(0)], joint.at[0])
    bring_image(0)

    def part_of(c):
        return pl.ds(c % 3 * width, width)

    def lift(c):
        if c == 0:
            have("down")
        have("d" + str(c))
        have("s" + str(c))

        @pl.loop(0, images)
        def _(image):
            line = pl.ds(pl.multiple_of(image * seq, seq), seq)
            value = times_back(mixed[line, :], stage[2])
            grad_joint[line, part_of(c)] = (value * grad_joint[line, part_of(c)].astype(jnp.float32)).astype(jnp.bfloat16)

        if c + 1 < chunks:
            bring_fc2(c + 1)
        else:
            for f in range(fsdp):
                fetch("proj", weight_ref.at[f, :, pl.ds(3 * width, width)], stage.at[2, pl.ds(f * rows, rows), :])

    def weigh_fc1(c):
        if c == 0:
            have("h2")
        else:
            have("e" + str(c - 1))

        @pl.loop(0, width // 128)
        def _(m):
            line = pl.ds(pl.multiple_of(m * 128, 128), 128)
            stage[1, line, :] = times_rows(h1[:, line], grad_joint[:, part_of(c)]).astype(jnp.bfloat16)

        store("e" + str(c), stage.at[1], expand_ref.at[:, pl.ds(c * width, width)], 6 + 2 * images + c)

    def grow(c):
        have("f" + str(c))

        @pl.loop(0, images)
        def _(image):
            line = pl.ds(pl.multiple_of(image * seq, seq), seq)
            value = times_back(grad_joint[line, part_of(c)], stage[0])
            if c == 0:
                total[line, :] = value
            else:
                total[line, :] = total[line, :] + value

        if c + 1 < chunks:
            bring_fc1(c + 1)
        if c + 3 < chunks:
            bring_slope(c + 3)
        if c == chunks - 2:
            fetch("forward", forward_ref, grad_joint.at[:, part_of(c)])
        if c == chunks - 1:
            have("e" + str(c))
            fetch("h1", h1_ref, h1)

    forward_at, grad_at, proj_at = (chunks - 2) % 3, (chunks - 1) % 3, 2

    def norm_two(image):
        have("image" + str(image))
        scale, gate = 1.0 + modulated(image, 4), modulated(image, 2)
        step = 32

        def chunk(i, sums):
            shift_sum, gain_sum, gate_sum = sums
            line = pl.ds(pl.multiple_of(image * seq + i * step, step), step)
            here = pl.ds(pl.multiple_of(i * step, step), step)
            value = middle[0, here, :]
            grad = total[line, :] + logit_ref[line, :] * pick_ref[...]
            centered = value - jnp.mean(value, axis=-1, keepdims=True)
            inverse = lax.rsqrt(jnp.mean(centered * centered, axis=-1, keepdims=True) + EPSILON)
            normed = centered * inverse
            through = grad * scale
            back = through - jnp.mean(through, axis=-1, keepdims=True)
            back = back - normed * jnp.mean(through * normed, axis=-1, keepdims=True)
            through = joint[1, here, :width].astype(jnp.float32) + inverse * back
            total[line, :] = through
            grad_joint[line, grad_at * width : (grad_at + 1) * width] = (through * gate).astype(jnp.bfloat16)
            return (
                shift_sum + jnp.sum(grad, axis=0, keepdims=True),
                gain_sum + jnp.sum(grad * normed, axis=0, keepdims=True),
                gate_sum + jnp.sum(through * middle[1, here, :], axis=0, keepdims=True),
            )

        zero = jnp.zeros((1, width), jnp.float32)
        shift, gain, gated = lax.fori_loop(0, seq // step, chunk, (zero, zero, zero))
        for index, row in ((2, gated), (3, shift), (4, gain)):
            gm_row[image : image + 1, index * width : (index + 1) * width] = row
        store("mid" + str(image), total.at[lines(image)], middle_ref.at[lines(image)], 3 + images + image)
        if image + 1 < images:
            bring_image(image + 1)

    def mix():
        have("proj")

        @pl.loop(0, images)
        def _(image):
            line = pl.ds(pl.multiple_of(image * seq, seq), seq)
            grad = grad_joint[line, grad_at * width : (grad_at + 1) * width]
            mixed[line, :] = times_back(grad, stage[proj_at]).astype(jnp.bfloat16)

    def weigh_proj():
        have("forward")

        @pl.loop(0, width // 128)
        def _(m):
            line = pl.ds(pl.multiple_of(m * 128, 128), 128)
            column = pl.ds(pl.multiple_of(forward_at * width + m * 128, 128), 128)
            value = times_rows(grad_joint[:, column], grad_joint[:, grad_at * width : (grad_at + 1) * width])
            stage[1, line, :] = value.astype(jnp.bfloat16)

        store("projected", stage.at[1], proj_ref, 3 + 2 * images)

    fetch("ada", ada_hbm, ada_ref)
    inner[...] = jnp.zeros_like(inner)
    gm_row[...] = jnp.zeros_like(gm_row)

    def attention(image, half):
        slot = image % 2
        if half == 0:
            have("joint" + str(image))
            if image + 1 < images:
                fetch("joint" + str(image + 1), joint_ref.at[lines(image + 1)], joint.at[1 - slot])
        span = range(0, heads // 2) if half == 0 else range(heads // 2, heads)
        attend_back_image(
            joint.at[slot], mixed.at[lines(image)], gates_ref, lse_ref, grad_joint.at[lines(image)], inner, image, seq, heads, span
        )

    def weigh(q):
        if q == 0:
            have("h1")
            have("projected")
            fetch("tokens", tokens_ref, mixed)
        slot = q % 2
        if q >= 2:
            have("out" + str(q - 2))

        @pl.loop(0, width // 128)
        def _(m):
            line = pl.ds(pl.multiple_of(m * 128, 128), 128)
            stage[slot, line, :] = times_rows(h1[:, line], grad_joint[:, pl.ds(q * width, width)]).astype(jnp.bfloat16)

        store("out" + str(q), stage.at[slot], triple_ref.at[q], q)

    def bring_weight(q):
        for f in range(fsdp):
            fetch("w" + str(q), weight_ref.at[f, :, pl.ds(q * width, width)], stage.at[q % 2, pl.ds(f * rows, rows), :])

    def wait_terms():
        for q in (1, 2):
            have("out" + str(q))
        for image in range(images):
            have("mid" + str(image))
        bring_weight(0)
        bring_weight(1)
        fetch("middle0", middle_ref.at[lines(0)], middle.at[0])

    def spread(q):
        slot = q % 2
        have("w" + str(q))

        @pl.loop(0, images)
        def _(image):
            line = pl.ds(pl.multiple_of(image * seq, seq), seq)
            value = times_back(grad_joint[line, pl.ds(q * width, width)], stage[slot])
            if q == 0:
                total[line, :] = value
            else:
                total[line, :] = total[line, :] + value

        if q == 0:
            bring_weight(2)

    def norm(image):
        slot = image % 2
        if image == 0:
            have("tokens")
        have("middle" + str(image))
        if image + 1 < images:
            if image >= 1:
                have("done" + str(image - 1))
            fetch("middle" + str(image + 1), middle_ref.at[lines(image + 1)], middle.at[1 - slot])
        scale = 1.0 + modulated(image, 1)
        step = 32

        def chunk(i, sums):
            shift, gain = sums
            line = pl.ds(pl.multiple_of(image * seq + i * step, step), step)
            here = pl.ds(pl.multiple_of(i * step, step), step)
            value = mixed[line, :].astype(jnp.float32)
            grad = total[line, :]
            centered = value - jnp.mean(value, axis=-1, keepdims=True)
            inverse = lax.rsqrt(jnp.mean(centered * centered, axis=-1, keepdims=True) + EPSILON)
            normed = centered * inverse
            through = grad * scale
            back = through - jnp.mean(through, axis=-1, keepdims=True)
            back = back - normed * jnp.mean(through * normed, axis=-1, keepdims=True)
            middle[slot, here, :] = middle[slot, here, :] + inverse * back
            return (
                shift + jnp.sum(grad, axis=0, keepdims=True),
                gain + jnp.sum(grad * normed, axis=0, keepdims=True),
            )

        zero = jnp.zeros((1, width), jnp.float32)
        shift, gain = lax.fori_loop(0, seq // step, chunk, (zero, zero))
        store("done" + str(image), middle.at[slot], grad_tokens_ref.at[lines(image)], 3 + image)
        gm_row[image : image + 1, :width] = shift
        gm_row[image : image + 1, width : 2 * width] = gain

    mates, cousins = at.mates(), at.cousins()
    swaps = [Swap(mates, mate_s.at[i], mate_r.at[i]) for i in range(3)]
    far = [Swap(cousins, cousin_s.at[i], cousin_r.at[i]) for i in range(2)]
    small = []

    def keep(src, dst):
        copy = pltpu.make_async_copy(src, dst, out_sem.at[4 + 2 * images + len(small)])
        copy.start()
        small.append(copy)

    held = gms.shape[3]

    def tail_zero():
        gm_row[:, 5 * width :] = gate_two_ref[...]
        for f in range(fsdp):
            gms[0, f] = gm_row[:, f * held : (f + 1) * held].astype(jnp.bfloat16)
        swaps[0].start(lambda device: gms.at[0, device[1]], gms.at[1, at.f])

    def tail_one():
        have("ada")
        swaps[0].arrived()
        gms[1, at.f] = gms[0, at.f]
        every = gms[1].astype(jnp.float32).reshape(fsdp * pad, held).astype(jnp.bfloat16)
        parts[...] = matmul(every, ada_ref[...]).reshape(parts.shape)
        swaps[1].start(lambda device: parts.at[device[1]], mine_in.at[at.f])
        far[0].start(lambda device: gms.at[1], all_gm_ref.at[at.d])
        keep(gms.at[1], all_gm_ref.at[at.d])

    def tail_two():
        line = lax.broadcasted_iota(jnp.int32, (pad, 128), 0)
        gated = jnp.zeros((pad, 128), jnp.float32)
        for image in range(images):
            summed = lax.dot_general(
                jnp.ones((pad, seq), jnp.float32), inner[image], (((1,), (1,)), ((), ())),
                preferred_element_type=jnp.float32, precision=lax.Precision.HIGHEST,
            )
            gated = jnp.where(line == image, summed, gated)
        router = (gated * factor_ref[...]).astype(jnp.bfloat16)
        swaps[1].arrived()
        mine_in[at.f] = parts[at.f]
        grad_cond = jnp.sum(mine_in[...], axis=0) + times_back(router, routers_ref[...])
        pre_cond = pre_ref[...]
        sig = jax.nn.sigmoid(pre_cond)
        grad_pre = grad_cond * (sig * (1.0 + pre_cond * (1.0 - sig)))
        pres[at.f, :, :width] = (grad_pre + picker_ref[...]).astype(jnp.bfloat16)
        pres[at.f, :, width:] = router
        swaps[2].start(lambda device: pres.at[at.f], pres.at[at.f])

    def tail_three():
        swaps[2].arrived()
        far[1].start(lambda device: pres, all_pre_ref.at[at.d])
        keep(pres, all_pre_ref.at[at.d])

    first = [partial(step, c) for c in range(chunks) for step in (lift, weigh_fc1, grow)]
    early = [partial(norm_two, image) for image in range(images)] + [mix, weigh_proj]
    early += [partial(attention, image, half) for image in range(images) for half in range(2)]
    early += [partial(weigh, q) for q in range(3)] + [wait_terms]
    norms = [partial(norm, image) for image in range(images)]
    late = [[partial(spread, q)] for q in range(3)] + [[step] for step in norms]
    late += [[tail_zero], [], [tail_one], [], [], [tail_two], [], [], [tail_three]]
    split = 4 * ring
    starts = (split // 2, split)

    def some(steps, t, turns):
        upto = [-(-len(steps) * (t + i) // turns) for i in range(2)]
        for step in steps[upto[0] : upto[1]]:
            step()

    for t in range(work.total + 4 * LAG):
        work.turn(t, starts)
        if t < split:
            some(first + early, t, split)
        elif t - split < len(late):
            for step in late[t - split]:
                step()
    for swap in far:
        swap.arrived()
    for copy in small:
        copy.wait()
    for image in range(max(images - 2, 0), images):
        have("done" + str(image))
    for swap in swaps + far:
        swap.left()
    work.finish()


def back_half(
    term_fc2, joint, flat_one, flat_two, tokens, joint_full, grad_down, slope, fc1_full, fc2_full, middle, attn, cotangent,
    mixed, log_total, gates, gate_two,
    modulation, factor, routers, ada_weight, pre_cond, picker, logit, pick, width, images, seq, dp, fsdp,
):
    rows = fc1_full.shape[1]
    heads = gates.shape[1]
    count = images * seq
    pad = pre_cond.shape[0]
    columns = ada_weight.shape[0]
    dma, vmem = pltpu.SemaphoreType.DMA, pltpu.VMEM
    low, f32 = jnp.bfloat16, jnp.float32
    out = jax.ShapeDtypeStruct
    any_space, in_vmem = pl.BlockSpec(memory_space=pl.ANY), pl.BlockSpec(memory_space=vmem)
    in_smem = pl.BlockSpec(memory_space=pltpu.SMEM)
    return pl.pallas_call(
        partial(back_kernel, dp, fsdp, width, images, seq, heads),
        out_shape=[out((QUARTERS, rows, width), low)] * 3
        + [
            out((dp, fsdp, pad, columns), low),
            out((dp, fsdp, pad, width + 128), low),
            out((count, width), f32),
            out((3, width, width), low),
            out((count, width), f32),
            out((width, width), low),
            out((width, fc1_full.shape[2]), low),
        ],
        in_specs=[any_space] * 14 + [in_vmem, in_smem] + [in_vmem] * 4 + [any_space] + [in_vmem] * 4,
        out_specs=[any_space] * 10,
        scratch_shapes=[
            vmem((2, seq, 3 * width), low),
            vmem((count, width), low),
            vmem((count, width), low),
            vmem((2, seq, width), f32),
            vmem((count, 3 * width), low),
            vmem((3, width, width), low),
            vmem((count, width), f32),
            vmem((images, 128, seq), f32),
            vmem((pad, 6 * width), f32),
            vmem((2, fsdp, pad, columns), low),
            vmem((fsdp, pad, width), f32),
            vmem((fsdp, pad, width), f32),
            vmem((fsdp, pad, width + 128), low),
            vmem(ada_weight.shape, low),
            dma((12 * fsdp + 12 + 5 * images,)),
            dma((6 + 2 * images + fc1_full.shape[2] // width,)),
            dma((3, fsdp - 1)),
            dma((3, fsdp - 1)),
            dma((2, dp - 1)),
            dma((2, dp - 1)),
        ]
        + Reducer.scratch(rows, width, fsdp),
        compiler_params=pltpu.CompilerParams(
            collective_id=1, has_side_effects=True, vmem_limit_bytes=60 * 2**20
        ),
        name="back",
    )(
        term_fc2, joint, flat_one, flat_two, tokens, joint_full, grad_down, slope, fc1_full, fc2_full, middle, attn,
        cotangent, mixed, log_total,
        gates[:, None, :], gate_two, modulation, factor, routers, ada_weight, pre_cond, picker, logit, pick,
    )


def body(
    dp,
    fsdp,
    tokens,
    timesteps,
    labels,
    head_mask,
    keep_mask,
    cotangent,
    time_weight,
    class_table,
    ada_weight,
    head_router,
    qkv_weight,
    proj_weight,
    fc1_weight,
    fc2_weight,
    token_router,
):
    images, seq, width = tokens.shape
    heads = head_mask.shape[1]
    count = images * seq
    rows = qkv_weight.shape[0]
    hidden = fc1_weight.shape[1]
    entries = time_weight.shape[0] * fsdp
    me_fsdp = lax.axis_index("fsdp")
    pad = -(-(images + 2) // 8) * 8

    def padded(array, value=0.0):
        return jnp.pad(array, ((0, pad - images), (0, 0)), constant_values=value)

    embedded = sinusoid(timesteps, entries).astype(jnp.bfloat16)
    digits = jnp.stack([labels // DIGIT, labels % DIGIT], axis=1).astype(jnp.bfloat16)
    asked = jnp.concatenate(
        [padded(embedded), jnp.pad(padded(digits, -1.0), ((0, 0), (0, 126)))], axis=1
    )
    routers = jnp.pad(
        jnp.concatenate([head_router, token_router], axis=1), ((0, 0), (0, 127 - heads))
    )
    mask_float = head_mask.astype(jnp.float32)
    *gathered, flat_one, joint, log_total, mixed, attn, middle, flat_two, active, slope, grad_down, grad_shrink = front_half(
        [
            jnp.concatenate([qkv_weight, proj_weight], axis=1),
            fc1_weight,
            fc2_weight.reshape(QUARTERS, rows, width),
        ],
        asked,
        time_weight,
        class_table.T,
        ada_weight.T,
        routers,
        padded(jnp.pad(mask_float, ((0, 0), (0, 128 - heads)))),
        tokens.reshape(count, width),
        keep_mask.astype(jnp.float32).reshape(count, 1),
        cotangent.reshape(count, width),
        width,
        images,
        seq,
        heads,
        dp,
        fsdp,
    )
    joint_blocks, fc1_full, fc2_full, pre_cond_pad, modulation_pad, routers_full, all_cond, all_asked = gathered
    shrink = fc2_full.reshape(hidden, width)
    routers_full = routers_full.reshape(width, 128)
    chooser, picker = routers_full[:, :heads], routers_full[:, heads : heads + 1]
    everyone = dp * fsdp * pad
    all_cond = all_cond.reshape(everyone, width)
    all_asked = all_asked.reshape(everyone, asked.shape[1])
    pre_cond = pre_cond_pad[:images]
    cond = jax.nn.silu(pre_cond).astype(jnp.bfloat16)
    gate_two = modulation_pad[:images, None, 5 * width :]
    router_sig = jax.nn.sigmoid(matmul(cond, chooser))
    head_gates = mask_float * router_sig
    middle = middle.reshape(images, seq, width)
    rate = jax.nn.sigmoid(matmul(flat_two, picker)).reshape(images, seq, 1)
    downward = matmul(active, shrink).reshape(images, seq, width)
    kept = keep_mask.astype(jnp.float32)[:, :, None]
    kept_rate = kept * rate
    output = (middle + gate_two * kept_rate * downward).astype(jnp.bfloat16)
    grad_out = cotangent.astype(jnp.float32)
    grad_gate_two = jnp.sum(grad_out * kept_rate * downward, axis=1)
    grad_rate = jnp.sum(grad_out * gate_two * downward, axis=-1, keepdims=True) * kept
    grad_logit = (grad_rate * rate * (1.0 - rate)).astype(jnp.bfloat16).reshape(count, 1)
    grad_picker = times_rows(grad_logit, flat_two)
    picker_high = lax.reduce_precision(grad_picker, 8, 7)
    *sums, all_grad, all_pre, grad_inputs, _, _, _, _ = back_half(
        grad_shrink.reshape(fsdp, QUARTERS, rows, width),
        joint,
        flat_one,
        flat_two,
        tokens.reshape(count, width),
        joint_blocks,
        grad_down,
        slope,
        fc1_full,
        fc2_full,
        middle.reshape(count, width),
        attn,
        cotangent.reshape(count, width),
        mixed,
        log_total,
        head_gates,
        padded(grad_gate_two),
        modulation_pad,
        padded(jnp.pad(mask_float * router_sig * (1.0 - router_sig), ((0, 0), (0, 128 - heads)))),
        routers_full,
        ada_weight.T,
        pre_cond_pad,
        jnp.pad(jnp.concatenate([picker_high, grad_picker - picker_high], axis=0), ((pad - 2, 0), (0, 0))),
        grad_logit.astype(jnp.float32),
        picker.astype(jnp.float32).reshape(1, width),
        width,
        images,
        seq,
        dp,
        fsdp,
    )
    grad_inputs = grad_inputs.reshape(images, seq, width)
    if dp > QUARTERS:
        parts = list(sums)
        for hop in range(QUARTERS, dp, QUARTERS):
            pairs = [(i, (i + hop) % dp) for i in range(dp)]
            parts = [
                part.astype(jnp.float32) + lax.ppermute(s, "dp", pairs).astype(jnp.float32)
                for part, s in zip(parts, sums)
            ]
        sums = parts
    sums = [s.astype(jnp.float32) for s in sums]
    sum_triple = jnp.concatenate([sums[2][0], sums[2][1], sums[2][2]], axis=1)
    sum_merger = sums[2][3]
    sum_expand = jnp.concatenate([sums[1][i] for i in range(QUARTERS)], axis=1)
    sum_shrink = sums[0].reshape(QUARTERS * rows, width)

    sum_ada = times_rows(all_cond, all_grad.reshape(everyone, -1))
    sum_picker = lax.dynamic_slice_in_dim(
        jnp.sum(all_pre[:, :, pad - 2 :, :width].astype(jnp.float32), axis=(0, 1, 2)), me_fsdp * rows, rows, axis=0
    )[:, None]
    is_image = (jnp.arange(pad) < images)[None, None, :, None]
    all_pre = jnp.where(is_image, all_pre, jnp.bfloat16(0.0)).reshape(everyone, -1)
    all_router = all_pre[:, width : width + heads]
    all_pre = all_pre[:, :width]
    own_entries = entries // fsdp
    all_embedded = lax.dynamic_slice_in_dim(
        all_asked[:, :entries], me_fsdp * own_entries, own_entries, axis=1
    )
    classes = jnp.arange(class_table.shape[0], dtype=jnp.float32)
    all_digits = all_asked[:, entries : entries + 2].astype(jnp.float32)
    all_labels = all_digits[:, :1] * DIGIT + all_digits[:, 1:]
    all_rows = (all_labels == classes[None, :]).astype(jnp.bfloat16)
    sum_time = times_rows(all_embedded, all_pre)
    sum_table = times_rows(
        all_rows, lax.dynamic_slice_in_dim(all_pre, me_fsdp * rows, rows, axis=1)
    )
    sum_chooser = times_rows(
        lax.dynamic_slice_in_dim(all_cond, me_fsdp * rows, rows, axis=1), all_router
    )
    return (
        output,
        grad_inputs,
        sum_time,
        sum_table,
        sum_ada,
        sum_chooser,
        sum_triple,
        sum_merger,
        sum_expand,
        sum_shrink,
        sum_picker,
    )


def solution(mesh):
    images = P(("dp", "fsdp"), None, None)
    pairs = P(("dp", "fsdp"), None)
    single = P(("dp", "fsdp"))
    by_row, by_column = P("fsdp", None), P(None, "fsdp")
    in_specs = (
        images, single, single, pairs, pairs, images,
        by_row, by_column, by_column, by_row, by_row, by_row, by_row, by_row, by_row,
    )
    out_specs = (
        images, images,
        by_row, by_column, by_column, by_row, by_row, by_row, by_row, by_row, by_row,
    )
    return jax.shard_map(
        partial(body, mesh.shape["dp"], mesh.shape["fsdp"]),
        mesh=mesh, in_specs=in_specs, out_specs=out_specs, check_vma=False,
    )
```

profile of v0, /device:TPU:0, one launch (start us, length us, event | category | flops | bytes accessed | tf_op | source)
XLA Modules:
  0.0 418.2 jit_solution(890367299199529499)
XLA Ops:
  0.6 0.7 convert_element_type.58
  1.4 0.7 convert_bitcast_fusion.2
  2.4 0.6 fusion.22.refs_3_
  3.0 0.7 convert_element_type.59
  4.3 0.7 convert_bitcast_fusion.1
  5.0 0.7 pad_maximum_fusion.3
  5.8 0.6 pad.41.refs_7_
  6.5 0.9 copy.49
  7.4 2.5 pad_maximum_fusion.2.refs_0_
  9.9 159.6 %front.1 = (bf16[8,144,4608]{2,1,0:T(8,128)(2,1)}, bf16[8,144,4608]{2,1,0:T(8,128)(2,1)}, bf16[8,4,144,1152]{3,2,1,0:T(8,128)(2,1)}, f32[8,1152]{1,0:T(8,128)}, ...) custom-call(bf16[144,4608]{1,0:T(8,128)(2,1)} %pad_maximum_fusion.2., ...), custom_call_target="tpu_custom_call" | custom-call | tf_op jit(solution)/shard_map/front/pallas_call | solution.py:489
  169.5 1.4 slice_reduce_fusion
  170.9 2.1 convolution_reduce_fusion.1
  173.1 1.1 subtract_multiply_fusion
  175.7 0.6 reshape.154.refs_24_
  176.3 0.8 slice.57
  177.1 17.2 %fusion.3 = (f32[3,256]{1,0:T(4,128)S(1)}, f32[3,1152]{1,0:T(4,128)S(1)}, bf16[3,256,1152]{2,1,0:T(8,128)(2,1)}) fusion(bf16[3,256,1152]{2,1,0:T(8,128)(2,1)S(1)} %copy-done.1, f32[3,1152]{1,0:T(4,128)S(1)} %slice.57, f32[3,256]{1,0:T(4,128)S(1)} %convert_multiply_fusion.2, f32[3,256,1152]{2,1,0:T(8,128)} %bitcast.81, bf16[3,256,4608]{2,1,0:T(8,128)(2,1)} %bitcast.99, ...), kind=kOutput, calls=%fused_computation.6 | convolution fusion | flops 8163454464 | bytes 24806400 | tf_op jit(solution)/shard_map/dot_general | solution.py:35
  194.7 0.6 select_maximum_fusion.refs_22_
  195.3 0.6 pad.44.refs_16_
  196.1 1.0 copy.52
  197.0 202.7 %back.1 = (bf16[4,144,1152]{2,1,0:T(8,128)(2,1)}, bf16[4,144,1152]{2,1,0:T(8,128)(2,1)}, bf16[4,144,1152]{2,1,0:T(8,128)(2,1)}, bf16[4,8,8,864]{3,2,1,0:T(8,128)...) custom-call(bf16[8,4,144,1152]{3,2,1,0:T(8,128)(2,1)} %bitcast.70, ...), custom_call_target="tpu_custom_call" | custom-call | tf_op jit(solution)/shard_map/back/pallas_call | solution.py:1256
  399.7 1.4 convert_reduce_fusion.1
  401.1 0.6 dynamic_slice.15
  401.8 1.2 broadcast_select_fusion
  403.0 1.0 fusion.14
  403.9 0.8 fusion.10
  404.8 1.2 fusion.7
  406.2 1.0 slice_bitcast_fusion.4
  407.3 1.4 pad_maximum_fusion.1
  409.6 1.8 pad_maximum_fusion
  411.4 1.8 bitcast_convert_fusion
  413.2 2.7 convolution_bitcast_fusion
  415.9 1.8 copy.54
  (57 shorter events, 4.3 us)
Async XLA Ops:
  9.9 163.2 %copy-start.10 = (s32[3,256]{1,0:T(4,128)S(1)}, s32[3,256]{1,0:T(4,128)}, u32[]{:S(2)}) copy-start(s32[3,256]{1,0:T(4,128)} %param.19) | copy-start | bytes 9220
  9.9 163.2 %copy-start.11 = (s32[3,16]{1,0:T(4,128)S(1)}, s32[3,16]{1,0:T(4,128)}, u32[]{:S(2)}) copy-start(s32[3,16]{1,0:T(4,128)} %param.18) | copy-start | bytes 580
  169.5 5.9 %copy-start.3 = (bf16[8,144,128]{2,1,0:T(8,128)(2,1)S(1)}, bf16[8,144,128]{2,1,0:T(8,128)(2,1)}, u32[]{:S(2)}) copy-start(bf16[8,144,128]{2,1,0:T(8,128)(2,1)} %get-tuple-element.39) | copy-start | bytes 884740
  169.5 7.5 %copy-start.1 = (bf16[3,256,1152]{2,1,0:T(8,128)(2,1)S(1)}, bf16[3,256,1152]{2,1,0:T(8,128)(2,1)}, u32[]{:S(2)}) copy-start(bf16[3,256,1152]{2,1,0:T(8,128)(2,1)} %param.20) | copy-start | bytes 5308420
  177.0 17.2 %copy-start = (bf16[768,1152]{1,0:T(8,128)(2,1)S(1)}, bf16[768,1152]{1,0:T(8,128)(2,1)}, u32[]{:S(2)}) copy-start(bf16[768,1152]{1,0:T(8,128)(2,1)} %get-tuple-element.38.refs_3_) | copy-start | bytes 5308420
  177.1 18.9 %copy-start.9 = (bf16[4,8,8,384]{3,2,1,0:T(8,128)(2,1)S(1)}, bf16[4,8,8,384]{3,2,1,0:T(8,128)(2,1)}, u32[]{:S(2)}) copy-start(bf16[4,8,8,384]{3,2,1,0:T(8,128)(2,1)} %get-tuple-element.54) | copy-start | bytes 589828
  197.0 206.9 %copy-start.7 = (bf16[4,8,8,1152]{3,2,1,0:T(8,128)(2,1)S(1)}, bf16[4,8,8,1152]{3,2,1,0:T(8,128)(2,1)}, u32[]{:S(2)}) copy-start(bf16[4,8,8,1152]{3,2,1,0:T(8,128)(2,1)} %get-tuple-element.56) | copy-start | bytes 1769476
  399.7 6.3 %copy-start.6 = (bf16[4,144,1152]{2,1,0:T(8,128)(2,1)S(1)}, bf16[4,144,1152]{2,1,0:T(8,128)(2,1)}, u32[]{:S(2)}) copy-start(bf16[4,144,1152]{2,1,0:T(8,128)(2,1)} %get-tuple-element.58) | copy-start | bytes 3981316
  407.3 2.0 copy-start.5
  409.6 1.8 copy-start.4
  411.4 1.8 copy-start.8
  413.2 2.7 copy-start.2
where the time goes:
time: 421 us; the launch traced here: 418 us
  Pallas kernels  362 us (86%)
  matrix products  26.5 us (6%)
  other arithmetic  15.6 us (4%)
  local copies, waits for them, and re-layouts  12.4 us (3%)
    pallas_call x1, Pallas kernels, back_half(): pl.pallas_call(partial(back_kernel, dp, fsdp, width, images, seq, heads),...  203 us
    pallas_call x1, Pallas kernels, front_half(): pl.pallas_call(partial(front_kernel, dp, fsdp, width, images, seq, heads)...  160 us
    dot_general x3, matrix products, matmul(): return jnp.dot(left, right, preferred_element_type=jnp.float32)  20.4 us

commit v1 on v0

--- a/solution.py
+++ b/solution.py
@@ -400,7 +400,7 @@
         landed[k].append(go(remote(shards[k], fulls[k].at[at.f], core_s.at[k, 0, 0], core_r.at[k, 0, 0], at.core)))
     flights = {}
     each = 2 * (ring - 1)
-    begin, second = each + 2 * LAG - 1, 2 * each + 2 * LAG
+    begin, second = each + 2 * LAG - 1, 2 * each + 2 * LAG - 1
     done = 0
     for turn in range(len(items) + 2 * LAG):
         if turn < len(items):

time: 421 us -> 417 us (level)
    pallas_call x1, Pallas kernels: 160 us -> 154 us  [front_half(): pl.pallas_call(partial(front_kernel, dp, fsdp, width, images, seq, heads)...]
where the time goes in v1:
time: 417 us; the launch traced here: 414 us
  Pallas kernels  358 us (86%)
  matrix products  26.5 us (6%)
  other arithmetic  15.6 us (4%)
  local copies, waits for them, and re-layouts  12.4 us (3%)
    pallas_call x1, Pallas kernels, back_half(): pl.pallas_call(partial(back_kernel, dp, fsdp, width, images, seq, heads),...  204 us
    pallas_call x1, Pallas kernels, front_half(): pl.pallas_call(partial(front_kernel, dp, fsdp, width, images, seq, heads)...  154 us
    dot_general x3, matrix products, matmul(): return jnp.dot(left, right, preferred_element_type=jnp.float32)  20.4 us

profile of v1, /device:TPU:0, one launch (start us, length us, event | category | flops | bytes accessed | tf_op | source)
XLA Modules:
  0.0 413.8 jit_solution(15331795300593485169)
XLA Ops:
  0.6 0.7 convert_element_type.58
  1.4 0.7 convert_bitcast_fusion.2
  2.4 0.6 fusion.22.refs_3_
  3.0 0.7 convert_element_type.59
  4.3 0.7 convert_bitcast_fusion.1
  5.0 0.7 pad_maximum_fusion.3
  5.8 0.6 pad.41.refs_7_
  6.5 0.9 copy.49
  7.4 2.5 pad_maximum_fusion.2.refs_0_
  9.9 154.2 %front.1 = (bf16[8,144,4608]{2,1,0:T(8,128)(2,1)}, bf16[8,144,4608]{2,1,0:T(8,128)(2,1)}, bf16[8,4,144,1152]{3,2,1,0:T(8,128)(2,1)}, f32[8,1152]{1,0:T(8,128)}, ...) custom-call(bf16[144,4608]{1,0:T(8,128)(2,1)} %pad_maximum_fusion.2., ...), custom_call_target="tpu_custom_call" | custom-call | tf_op jit(solution)/shard_map/front/pallas_call | solution.py:489
  164.1 1.4 slice_reduce_fusion
  165.5 2.1 convolution_reduce_fusion.1
  167.6 1.1 subtract_multiply_fusion
  170.3 0.6 reshape.154.refs_24_
  170.9 0.8 slice.57
  171.6 17.2 %fusion.3 = (f32[3,256]{1,0:T(4,128)S(1)}, f32[3,1152]{1,0:T(4,128)S(1)}, bf16[3,256,1152]{2,1,0:T(8,128)(2,1)}) fusion(bf16[3,256,1152]{2,1,0:T(8,128)(2,1)S(1)} %copy-done.1, f32[3,1152]{1,0:T(4,128)S(1)} %slice.57, f32[3,256]{1,0:T(4,128)S(1)} %convert_multiply_fusion.2, f32[3,256,1152]{2,1,0:T(8,128)} %bitcast.81, bf16[3,256,4608]{2,1,0:T(8,128)(2,1)} %bitcast.99, ...), kind=kOutput, calls=%fused_computation.6 | convolution fusion | flops 8163454464 | bytes 24806400 | tf_op jit(solution)/shard_map/dot_general | solution.py:35
  189.2 0.6 select_maximum_fusion.refs_22_
  189.9 0.6 pad.44.refs_16_
  190.6 1.0 copy.52
  191.6 203.7 %back.1 = (bf16[4,144,1152]{2,1,0:T(8,128)(2,1)}, bf16[4,144,1152]{2,1,0:T(8,128)(2,1)}, bf16[4,144,1152]{2,1,0:T(8,128)(2,1)}, bf16[4,8,8,864]{3,2,1,0:T(8,128)...) custom-call(bf16[8,4,144,1152]{3,2,1,0:T(8,128)(2,1)} %bitcast.70, ...), custom_call_target="tpu_custom_call" | custom-call | tf_op jit(solution)/shard_map/back/pallas_call | solution.py:1256
  395.3 1.4 convert_reduce_fusion.1
  396.7 0.6 dynamic_slice.15
  397.3 1.2 broadcast_select_fusion
  398.5 1.0 fusion.14
  399.5 0.8 fusion.10
  400.4 1.2 fusion.7
  401.8 1.0 slice_bitcast_fusion.4
  402.8 1.4 pad_maximum_fusion.1
  405.2 1.8 pad_maximum_fusion
  407.0 1.8 bitcast_convert_fusion
  408.7 2.7 convolution_bitcast_fusion
  411.5 1.8 copy.54
  (57 shorter events, 4.3 us)
Async XLA Ops:
  9.9 157.7 %copy-start.10 = (s32[3,256]{1,0:T(4,128)S(1)}, s32[3,256]{1,0:T(4,128)}, u32[]{:S(2)}) copy-start(s32[3,256]{1,0:T(4,128)} %param.19) | copy-start | bytes 9220
  9.9 157.8 %copy-start.11 = (s32[3,16]{1,0:T(4,128)S(1)}, s32[3,16]{1,0:T(4,128)}, u32[]{:S(2)}) copy-start(s32[3,16]{1,0:T(4,128)} %param.18) | copy-start | bytes 580
  164.1 5.9 %copy-start.3 = (bf16[8,144,128]{2,1,0:T(8,128)(2,1)S(1)}, bf16[8,144,128]{2,1,0:T(8,128)(2,1)}, u32[]{:S(2)}) copy-start(bf16[8,144,128]{2,1,0:T(8,128)(2,1)} %get-tuple-element.39) | copy-start | bytes 884740
  164.1 7.5 %copy-start.1 = (bf16[3,256,1152]{2,1,0:T(8,128)(2,1)S(1)}, bf16[3,256,1152]{2,1,0:T(8,128)(2,1)}, u32[]{:S(2)}) copy-start(bf16[3,256,1152]{2,1,0:T(8,128)(2,1)} %param.20) | copy-start | bytes 5308420
  171.6 17.2 %copy-start = (bf16[768,1152]{1,0:T(8,128)(2,1)S(1)}, bf16[768,1152]{1,0:T(8,128)(2,1)}, u32[]{:S(2)}) copy-start(bf16[768,1152]{1,0:T(8,128)(2,1)} %get-tuple-element.38.refs_3_) | copy-start | bytes 5308420
  171.6 18.9 %copy-start.9 = (bf16[4,8,8,384]{3,2,1,0:T(8,128)(2,1)S(1)}, bf16[4,8,8,384]{3,2,1,0:T(8,128)(2,1)}, u32[]{:S(2)}) copy-start(bf16[4,8,8,384]{3,2,1,0:T(8,128)(2,1)} %get-tuple-element.54) | copy-start | bytes 589828
  191.6 207.9 %copy-start.7 = (bf16[4,8,8,1152]{3,2,1,0:T(8,128)(2,1)S(1)}, bf16[4,8,8,1152]{3,2,1,0:T(8,128)(2,1)}, u32[]{:S(2)}) copy-start(bf16[4,8,8,1152]{3,2,1,0:T(8,128)(2,1)} %get-tuple-element.56) | copy-start | bytes 1769476
  395.3 6.3 %copy-start.6 = (bf16[4,144,1152]{2,1,0:T(8,128)(2,1)S(1)}, bf16[4,144,1152]{2,1,0:T(8,128)(2,1)}, u32[]{:S(2)}) copy-start(bf16[4,144,1152]{2,1,0:T(8,128)(2,1)} %get-tuple-element.58) | copy-start | bytes 3981316
  402.8 2.0 copy-start.5
  405.1 1.8 copy-start.4
  407.0 1.8 copy-start.8
  408.7 2.7 copy-start.2
